TPU v7x, 128 devices: a whole 4x4x4 slice. The times are simulated.
128 devices in a mesh: ctx: 8 (over x_hi, y), head: 8 (over z, core), var: 2 (over x_lo).
Axes of the slice: x: 4 (x_hi: 2, x_lo: 2; x = x_hi * 2 + x_lo), y: 4, z: 4, core: 2. Of those that a mesh axis runs over, the one named last changes fastest.
Arguments:
- sequence: bfloat16 [4096, 1536], P('ctx', 'head'), may hold values from -8 to 8
- deletions: int32 [8, 2], P('var'), parts along dimension 0, may hold values from 0 to 4096, as said below
- conv_taps: float32 [3, 1536], P(None, 'head'), may hold values from -3 to 3
- conv_bias: float32 [1536], P('head'), may hold values from -3 to 3
- w_proj: bfloat16 [1536, 3584], P(None, 'head'), may hold values from -1 to 1
- w_out: bfloat16 [1536, 1536], P('head'), may hold values from -0.15625 to 0.15625
- w_pair: bfloat16 [1536, 256], P('head'), may hold values from -0.15625 to 0.15625
- dist_table: float32 [16, 128], replicated, may hold values from -3 to 3
Outputs:
- pair_map: bfloat16 [8, 1024, 1024, 128], P('var', 'ctx', 'head'), parts along dimension 0
There are 2 independent parts, one for each index of `var`. A program takes and returns all parts, laid end to end along the dimension named above; an argument that names none is the same for every part. Nothing has to cross between parts.
Inputs may be any that keep to these rules, and one draw needn't show every extreme that they name: `deletions`: each variant deletes 1 to 128 consecutive tokens, some variant deletes exactly 128, and some variant's deletion ends at the last token of the locus.
All inputs are finite; a program needn't handle non-finite values.
Results may differ from a plain program's by a relative error of at most 0.025.
Values may be sent and summed in bfloat16 or wider, within the bound.
A program may use at most 128 MiB of HBM per device.

v0:
```python
import math
import jax
import jax.numpy as jnp
from jax import lax
from jax.sharding import PartitionSpec as P

HD = 128
VD = 192
C = 128
NB = 16
POOL = 4


def extended(block, sides, width):
    for axis, dim in sides:
        count = lax.axis_size(axis)
        forward = [(i, i + 1) for i in range(count - 1)]
        backward = [(target, source) for source, target in forward]
        low = lax.ppermute(
            lax.slice_in_dim(block, block.shape[dim] - width, None, axis=dim), axis, forward
        )
        high = lax.ppermute(lax.slice_in_dim(block, 0, width, axis=dim), axis, backward)
        block = jnp.concatenate([low, block, high], axis=dim)
    return block


def attend_block(running, queries, key_rows, value_rows):
    row_max, row_sum, weighted = running
    scores = jnp.einsum(
        "vqhe,vkhe->vhqk", queries, key_rows, preferred_element_type=jnp.float32
    ) / math.sqrt(queries.shape[-1])
    new_max = jnp.maximum(row_max, scores.max(-1))
    shrink = jnp.exp(row_max - new_max)
    weights = jnp.exp(scores - new_max[..., None])
    row_sum = row_sum * shrink + weights.sum(-1)
    weighted = weighted * shrink[..., None] + jnp.einsum(
        "vhqk,vkhe->vhqe",
        weights.astype(jnp.bfloat16),
        value_rows,
        preferred_element_type=jnp.float32,
    )
    return (new_max, row_sum, weighted)


def attend_rows(running, queries, key_rows, value_rows):
    key_total = key_rows.shape[1]
    block_rows = 512
    block_count = key_total // block_rows

    def block_step(block_index, state_now):
        key_part = lax.dynamic_slice_in_dim(key_rows, block_index * block_rows, block_rows, 1)
        value_part = lax.dynamic_slice_in_dim(value_rows, block_index * block_rows, block_rows, 1)
        return attend_block(state_now, queries, key_part, value_part)

    return lax.fori_loop(0, block_count, block_step, running)


def local(sequence, deletions, conv_taps, conv_bias, w_proj, w_out, w_pair, dist_table):
    token_count, local_width = sequence.shape
    variants = deletions.shape[0]
    head_count = w_out.shape[0] // VD
    row_start = lax.axis_index("ctx") * token_count
    positions = row_start + jnp.arange(token_count, dtype=jnp.int32)
    kept = jnp.logical_or(
        positions[None, :] < deletions[:, 0:1], positions[None, :] >= deletions[:, 1:2]
    )
    masked = jnp.where(kept[:, :, None], sequence[None], jnp.zeros((), jnp.bfloat16))
    dilation = token_count // 2
    padded = extended(masked, (("ctx", 1),), dilation)
    spread = padded.astype(jnp.float32)
    middle = spread[:, dilation : dilation + token_count]
    convolved = (
        conv_taps[0] * spread[:, :token_count]
        + conv_taps[1] * middle
        + conv_taps[2] * spread[:, 2 * dilation : 2 * dilation + token_count]
        + conv_bias
    )
    trunk_out = (middle + jax.nn.gelu(convolved, approximate=True)).astype(jnp.bfloat16)
    projected = jnp.einsum(
        "vtd,df->vtf",
        lax.all_gather(trunk_out, "head", axis=2, tiled=True),
        w_proj,
        preferred_element_type=jnp.float32,
    ).astype(jnp.bfloat16)
    projected = projected.reshape(trunk_out.shape[0], token_count, head_count, 2 * HD + VD)
    queries = projected[:variants, :, :, :HD]
    key_rows = projected[:, :, :, HD : 2 * HD]
    value_rows = projected[:, :, :, 2 * HD :]
    running = attend_rows(
        (
            jnp.full((variants, head_count, token_count), -jnp.inf, jnp.float32),
            jnp.zeros((variants, head_count, token_count), jnp.float32),
            jnp.zeros((variants, head_count, token_count, VD), jnp.float32),
        ),
        queries,
        lax.all_gather(key_rows, "ctx", axis=1, tiled=True),
        lax.all_gather(value_rows, "ctx", axis=1, tiled=True),
    )
    row_max, row_sum, weighted = running
    head_out = (weighted / row_sum[..., None]).astype(jnp.bfloat16)
    flat_out = head_out.transpose(0, 2, 1, 3).reshape(variants * token_count, head_count * VD)
    mixed_back = lax.psum_scatter(
        lax.dot_general(
            w_out, flat_out, (((0,), (1,)), ((), ())), preferred_element_type=jnp.float32
        ).astype(jnp.bfloat16),
        "head",
        scatter_dimension=0,
        tiled=True,
    ).astype(jnp.float32)
    residual = trunk_out.astype(jnp.float32) + mixed_back.T.reshape(
        variants, token_count, local_width
    )
    pooled = (
        residual.reshape(variants, token_count // POOL, POOL, local_width)
        .mean(2)
        .astype(jnp.bfloat16)
    )
    partial_value = jnp.einsum("vpd,dc->vpc", pooled, w_pair, preferred_element_type=jnp.float32)
    pair_proj = lax.psum(partial_value.astype(jnp.bfloat16), "head").astype(jnp.float32)
    row_feats = pair_proj[:, :, :C]
    all_cols = lax.all_gather(
        pair_proj[:, :, C:].astype(jnp.bfloat16), "ctx", axis=1, tiled=True
    ).astype(jnp.float32)
    col_count = all_cols.shape[1] // lax.axis_size("head")
    col_start = lax.axis_index("head") * col_count
    col_feats = lax.dynamic_slice_in_dim(all_cols, col_start, col_count, 1)
    row_ids = lax.axis_index("ctx") * (token_count // POOL) + jnp.arange(
        token_count // POOL, dtype=jnp.int32
    )
    col_ids = col_start + jnp.arange(col_count, dtype=jnp.int32)
    distance = jnp.abs(row_ids[:, None] - col_ids[None, :])
    buckets = jnp.zeros(distance.shape, jnp.int32)
    for power_index in range(NB - 1):
        buckets = buckets + (distance >= 2**power_index).astype(jnp.int32)
    one_hot = (buckets[:, :, None] == jnp.arange(NB, dtype=jnp.int32)).astype(jnp.float32)
    rel_table = jnp.dot(one_hot, dist_table, precision=lax.Precision.HIGHEST)
    pair_map = row_feats[:, :, None, :] + col_feats[:, None, :, :] + rel_table[None]
    return pair_map.astype(jnp.bfloat16)


def solution(mesh):
    in_specs = (
        P("ctx", "head"),
        P("var", None),
        P(None, "head"),
        P("head"),
        P(None, "head"),
        P("head", None),
        P("head", None),
        P(),
    )
    out_specs = P("var", "ctx", "head", None)
    return jax.shard_map(local, mesh=mesh, in_specs=in_specs, out_specs=out_specs, check_vma=False)
```

profile of v0, /device:TPU:0, one launch (start us, length us, event | category | flops | bytes accessed | tf_op | source)
XLA Modules:
  0.0 486.1 jit_solution(6132765217847577570)
XLA Ops:
  8.5 3.6 collective-permute-start
  13.4 7.0 %collective-permute-done = bf16[4,256,192]{1,2,0:T(8,128)(2,1)S(1)} collective-permute-done((bf16[4,256,192]{1,2,0:T(8,128)(2,1)S(1)}, bf16[4,256,192]{1,2,0:T(8,128)(2,1)S(1)}, u32[]{:S(2)}, u32[]{:S(2)}) %collective-permute-start) | collective-permute-done | bytes 393248 | tf_op jit(solution)/shard_map/ppermute | solution.py:19
  20.4 4.1 collective-permute-done.1
  28.8 45.7 %all-gather.5.cloned.1.call-done = bf16[4,512,1536]{1,2,0:T(8,128)(2,1)} async-done(((bf16[4,512,192]{1,2,0:T(8,128)(2,1)}), bf16[4,512,1536]{1,2,0:T(8,128)(2,1)}) %all-gather.5.cloned.1.call-update) | async-done | bytes 6291472 | tf_op jit(solution)/shard_map/all_gather | solution.py:81
  74.5 5.8 %convert_bitcast_fusion = bf16[4,512,1,448]{1,3,0,2:T(8,128)(2,1)S(1)} fusion(bf16[4,512,1536]{1,2,0:T(8,128)(2,1)} %all-gather.5.cloned.1.call-done, bf16[1536,448]{0,1:T(8,128)(2,1)S(1)} %copy-done), kind=kOutput, calls=%fused_computation.29 | convolution fusion | flops 2819489792 | bytes 9502720 | tf_op jit(solution)/shard_map/vtd,df->vtf/dot_general | solution.py:79
  85.0 71.1 %all-gather.7.cloned.1.call-done = bf16[4,4096,1,128]{1,3,0,2:T(8,128)(2,1)} async-done(((bf16[4,512,1,128]{1,3,0,2:T(8,128)(2,1)}), bf16[4,4096,1,128]{1,3,0,2:T(8,128)(2,1)}) %all-gather.7.cloned.1.call-update) | async-done | bytes 4194320 | tf_op jit(solution)/shard_map/all_gather | solution.py:96
  156.1 93.5 %all-gather.9.cloned.1.call-done = bf16[4,4096,1,192]{1,3,0,2:T(8,128)(2,1)} async-done(((bf16[4,512,1,192]{1,3,0,2:T(8,128)(2,1)}), bf16[4,4096,1,192]{1,3,0,2:T(8,128)(2,1)}) %all-gather.9.cloned.1.call-update) | async-done | bytes 6291472 | tf_op jit(solution)/shard_map/all_gather | solution.py:97
  249.6 40.1 %while.18 = (s32[]{:T(128)}, f32[4,1,512]{2,0,1:T(4,128)S(1)}, f32[4,1,512]{2,0,1:T(4,128)S(1)}, f32[4,1,512,192]{2,3,0,1:T(8,128)S(1)}, bf16[4,4096,1,128]{1,3,...) while((s32[]{:T(128)}, f32[4,1,512]{2,0,1:T(4,128)S(1)}, ...), condition=%wide.region_3.4_spmd.clone, body=%wide.region_0.3_spmd.clone.sunk | while | flops 680669184 | bytes 17694904 | solution.py:55
  252.1 2.4 bitcast_add_fusion.5
  257.1 2.4 bitcast_add_fusion.5
  262.2 2.4 bitcast_add_fusion.5
  267.2 2.4 bitcast_add_fusion.5
  272.2 2.4 bitcast_add_fusion.5
  277.2 2.4 bitcast_add_fusion.5
  287.3 2.4 bitcast_add_fusion.5
  291.0 4.5 fusion.19
  295.6 8.7 %copy.38 = bf16[1536,2048]{1,0:T(8,128)(2,1)} copy(bf16[1536,2048]{0,1:T(8,128)(2,1)} %fusion.19) | data formatting | bytes 12582912
  304.5 40.6 %reduce-scatter.4.cloned.1.call-done = bf16[192,2048]{1,0:T(8,128)(2,1)} async-done(((bf16[1536,2048]{1,0:T(8,128)(2,1)}), bf16[192,2048]{1,0:T(8,128)(2,1)}) %reduce-scatter.4.cloned.1.call-update) | async-done | bytes 786448
  348.0 2.9 copy.32
  351.0 3.6 convert_add_fusion
  358.5 59.7 %all-reduce.2.cloned.1.call-done = bf16[4,128,256]{2,1,0:T(8,128)(2,1)} async-done(((bf16[4,128,256]{2,1,0:T(8,128)(2,1)}), bf16[4,128,256]{2,1,0:T(8,128)(2,1)}) %all-reduce.2.cloned.1.call-update) | async-done | bytes 262160 | tf_op jit(solution)/shard_map/psum | solution.py:119
  420.1 8.9 %fusion.33 = f32[128,128,128]{2,1,0:T(8,128)} fusion(s32[128,128]{1,0:T(8,128)S(1)} %convert_add_fusion.1, f32[16,128]{1,0:T(8,128)S(1)} %copy-done.7), kind=kOutput, calls=%fused_computation.50 | convolution fusion | flops 402915328 | bytes 8462336 | tf_op jit(solution)/shard_map/dot_general | solution.py:136
  429.0 36.8 %all-gather.11.cloned.1.call-done = bf16[4,1024,128]{2,1,0:T(8,128)(2,1)} async-done(((bf16[4,128,128]{2,1,0:T(8,128)(2,1)}), bf16[4,1024,128]{2,1,0:T(8,128)(2,1)}) %all-gather.11.cloned.1.call-update) | async-done | bytes 1048592 | tf_op jit(solution)/shard_map/all_gather | solution.py:121
  466.8 12.4 %add_convert_fusion = bf16[4,128,128,128]{3,2,1,0:T(8,128)(2,1)} fusion(f32[128,128,128]{2,1,0:T(8,128)} %fusion.33, f32[4,128,128]{2,1,0:T(8,128)S(1)} %dynamic-slice_convert_fusion, f32[4,128,128]{2,1,0:T(8,128)S(1)} %get-tuple-element.206), kind=kLoop, calls=%fused_computation.24 | loop fusion | flops 25165824 | bytes 25690112 | tf_op jit(solution)/shard_map/convert_element_type | solution.py:138
  (101 shorter events, 46.0 us)
Async XLA Ops:
  6.5 68.0 %copy-start = (bf16[1536,448]{0,1:T(8,128)(2,1)S(1)}, bf16[1536,448]{0,1:T(8,128)(2,1)}, u32[]{:S(2)}) copy-start(bf16[1536,448]{0,1:T(8,128)(2,1)} %param.14) | copy-start | bytes 4128772
  6.5 6.9 %copy-start.9 = (f32[3,192]{1,0:T(4,128)S(1)}, f32[3,192]{1,0:T(4,128)}, u32[]{:S(2)}) copy-start(f32[3,192]{1,0:T(4,128)} %param.12) | copy-start | bytes 6916
  6.5 68.0 %all-gather.5.cloned.1.call-start = ((), (), s32[]{:S(2)}) async-start(), calls=%async_computation.1 | async-start | bytes 7077888 | tf_op jit(solution)/shard_map/all_gather | solution.py:81
  8.5 11.9 %collective-permute-start = (bf16[4,256,192]{1,2,0:T(8,128)(2,1)S(1)}, bf16[4,256,192]{1,2,0:T(8,128)(2,1)S(1)}, u32[]{:S(2)}, u32[]{:S(2)}) collective-permute-start(bf16[4,256,192]{1,2,0:T(8,128)(2,1)S(1)} %get-tuple-element.204), channel_id=1, source_target_pairs={{0,16},{16,32},{32,48},{48,64},{64,80},{80,96},{96,112},{1,17},{17... | collective-permute-start | bytes 1179656 | tf_op jit(solution)/shard_map/ppermute | solution.py:19
  12.1 12.5 %collective-permute-start.1 = (bf16[4,256,192]{1,2,0:T(8,128)(2,1)S(1)}, bf16[4,256,192]{1,2,0:T(8,128)(2,1)S(1)}, u32[]{:S(2)}, u32[]{:S(2)}) collective-permute-start(bf16[4,256,192]{1,2,0:T(8,128)(2,1)S(1)} %get-tuple-element.205), channel_id=1, source_target_pairs={{16,0},{32,16},{48,32},{64,48},{80,64},{96,80},{112,96},{17,1},{33... | collective-permute-start | bytes 1179656 | tf_op jit(solution)/shard_map/ppermute | solution.py:22
  13.4 13.4 %copy-start.8 = (f32[192]{0:T(256)S(1)}, f32[192]{0:T(256)}, u32[]{:S(2)}) copy-start(f32[192]{0:T(256)} %param.13) | copy-start | bytes 2308
  25.0 1.8 copy-start.2
  28.8 127.3 %all-gather.7.cloned.1.call-start = ((), (), s32[]{:S(2)}) async-start(), calls=%async_computation.2 | async-start | bytes 4718592 | tf_op jit(solution)/shard_map/all_gather | solution.py:96
  80.3 1.2 copy-start.4
  82.4 167.1 %all-gather.9.cloned.1.call-start = ((), (), s32[]{:S(2)}) async-start(), calls=%async_computation.3 | async-start | bytes 7077888 | tf_op jit(solution)/shard_map/all_gather | solution.py:97
  84.6 260.5 %reduce-scatter.4.cloned.1.call-start = ((), (), s32[]{:S(2)}) async-start(), calls=%async_computation.6 | async-start | bytes 7077888
  289.9 1.1 copy-start.5
  304.3 113.9 %all-reduce.2.cloned.1.call-start = ((), (), s32[]{:S(2)}) async-start(), calls=%async_computation.4 | async-start | bytes 524288 | tf_op jit(solution)/shard_map/psum | solution.py:119
  348.0 2.9 copy-start.3
  356.6 0.9 copy-start.6
  357.2 63.0 %copy-start.7 = (f32[16,128]{1,0:T(8,128)S(1)}, f32[16,128]{1,0:T(8,128)}, u32[]{:S(2)}) copy-start(f32[16,128]{1,0:T(8,128)} %param.17) | copy-start | bytes 24580
  358.5 107.4 %all-gather.11.cloned.1.call-start = ((), (), s32[]{:S(2)}) async-start(), calls=%async_computation.5 | async-start | bytes 1179648 | tf_op jit(solution)/shard_map/all_gather | solution.py:121
  466.8 12.4 %copy-start.1 = (bf16[1536,448]{0,1:T(8,128)(2,1)S(1)}, bf16[1536,448]{0,1:T(8,128)(2,1)}, u32[]{:S(2)}) copy-start(bf16[1536,448]{0,1:T(8,128)(2,1)} %param.14) | copy-start | bytes 4128772
Sparse Core Ops, SparseCore 0:
  28.9 45.5 all-gather.4
  82.6 73.4 all-gather.6
  158.3 91.2 all-gather.8
  304.4 40.6 reduce-scatter.3
  358.6 59.6 all-reduce.1
  420.7 45.1 all-gather.10
where the time goes:
time: 488 us; the launch traced here: 486 us
  waiting for transfers between devices  359 us (74%)
  matrix products  54 us (11%)
  other arithmetic  30.4 us (6%)
  local copies, waits for them, and re-layouts  23.6 us (5%)
  between operations  13.7 us (3%)
  starting transfers between devices  5.27 us (1%)
    all_gather x1, waiting for transfers between devices, local(): lax.all_gather(value_rows, 'ctx', axis=1, tiled=True)  93.5 us
    all_gather x1, waiting for transfers between devices, local(): lax.all_gather(key_rows, 'ctx', axis=1, tiled=True)  71.1 us
    psum x1, waiting for transfers between devices, local(): lax.psum(partial_value.astype(jnp.bfloat16), 'head').astype(jnp.float32)  59.7 us
    all_gather x1, waiting for transfers between devices, local(): lax.all_gather(trunk_out, 'head', axis=2, tiled=True)  45.7 us
    unnamed x7, waiting for transfers between devices  40.6 us
    all_gather x1, waiting for transfers between devices, local(): lax.all_gather(pair_proj[:, :, C:].astype(jnp.bfloat16), 'ctx', axis=1, t...  36.8 us
    dot_general x8, matrix products, attend_block(): jnp.einsum('vhqk,vkhe->vhqe', weights.astype(jnp.bfloat16), value_rows, p...  19.3 us
    dot_general x8, matrix products, attend_block(): jnp.einsum('vqhe,vkhe->vhqk', queries, key_rows, preferred_element_type=j...  14.5 us
  transfers between devices with their start and end apart: 8, of which 8 were waited for; matrix products, arithmetic and copies ran while one was open for 2% of the time, Pallas kernels for 0%

commit v1 on v0

--- a/solution.py
+++ b/solution.py
@@ -93,7 +93,9 @@
             jnp.zeros((variants, head_count, token_count, VD), jnp.float32),
         ),
         queries,
-        lax.all_gather(key_rows, "ctx", axis=1, tiled=True),
+        jnp.concatenate(
+            lax.all_to_all(jnp.stack([key_rows] * lax.axis_size("ctx")), "ctx", 0, 0), axis=1
+        ),
         lax.all_gather(value_rows, "ctx", axis=1, tiled=True),
     )
     row_max, row_sum, weighted = running

time: 488 us -> 454 us (0.930)
  waiting for transfers between devices: 359 us -> 311 us
  local copies, waits for them, and re-layouts: 23.6 us -> 30.7 us
  starting transfers between devices: 5.27 us -> 11.9 us
    all_gather x1 -> x0, waiting for transfers between devices: 71.1 us -> none  [local(): lax.all_gather(key_rows, 'ctx', axis=1, tiled=True)]
    all_to_all x0 -> x1, waiting for transfers between devices: none -> 56.4 us  [local(): lax.all_to_all(jnp.stack([key_rows] * lax.axis_size('ctx')), 'ctx', 0, 0)]
    all_gather x1, waiting for transfers between devices: 93.5 us -> 60.9 us  [local(): lax.all_gather(value_rows, 'ctx', axis=1, tiled=True)]
    all_to_all x0 -> x1, starting transfers between devices: none -> 6.7 us  [local(): lax.all_to_all(jnp.stack([key_rows] * lax.axis_size('ctx')), 'ctx', 0, 0)]
    unnamed x7 -> x6, waiting for transfers between devices: 40.6 us -> 40.6 us
  transfers between devices with their start and end apart: 8 -> 8, of which waited for: 8 -> 8; matrix products, arithmetic and copies ran while one was open for 2% -> 4% of each run, Pallas kernels for 0% -> 0%
where the time goes in v1:
time: 454 us; the launch traced here: 452 us
  waiting for transfers between devices  311 us (69%)
  matrix products  53.7 us (12%)
  local copies, waits for them, and re-layouts  30.7 us (7%)
  other arithmetic  30.4 us (7%)
  between operations  13.4 us (3%)
  starting transfers between devices  11.9 us (3%)
    all_gather x1, waiting for transfers between devices, local(): lax.all_gather(value_rows, 'ctx', axis=1, tiled=True)  60.9 us
    psum x1, waiting for transfers between devices, local(): lax.psum(partial_value.astype(jnp.bfloat16), 'head').astype(jnp.float32)  59.8 us
    all_to_all x1, waiting for transfers between devices, local(): lax.all_to_all(jnp.stack([key_rows] * lax.axis_size('ctx')), 'ctx', 0, 0)  56.4 us
    all_gather x1, waiting for transfers between devices, local(): lax.all_gather(trunk_out, 'head', axis=2, tiled=True)  45.7 us
    unnamed x6, waiting for transfers between devices  40.6 us
    all_gather x1, waiting for transfers between devices, local(): lax.all_gather(pair_proj[:, :, C:].astype(jnp.bfloat16), 'ctx', axis=1, t...  36.8 us
    dot_general x8, matrix products, attend_block(): jnp.einsum('vhqk,vkhe->vhqe', weights.astype(jnp.bfloat16), value_rows, p...  19.4 us
    dot_general x8, matrix products, attend_block(): jnp.einsum('vqhe,vkhe->vhqk', queries, key_rows, preferred_element_type=j...  14.2 us
  transfers between devices with their start and end apart: 8, of which 8 were waited for; matrix products, arithmetic and copies ran while one was open for 4% of the time, Pallas kernels for 0%

profile of v1, /device:TPU:0, one launch (start us, length us, event | category | flops | bytes accessed | tf_op | source)
XLA Modules:
  0.0 451.9 jit_solution(16074030588416954691)
XLA Ops:
  8.5 3.6 collective-permute-start
  13.4 7.0 %collective-permute-done = bf16[4,256,192]{1,2,0:T(8,128)(2,1)S(1)} collective-permute-done((bf16[4,256,192]{1,2,0:T(8,128)(2,1)S(1)}, bf16[4,256,192]{1,2,0:T(8,128)(2,1)S(1)}, u32[]{:S(2)}, u32[]{:S(2)}) %collective-permute-start) | collective-permute-done | bytes 393248 | tf_op jit(solution)/shard_map/ppermute | solution.py:19
  20.4 4.1 collective-permute-done.1
  28.8 45.7 %all-gather.4.cloned.1.call-done = bf16[4,512,1536]{1,2,0:T(8,128)(2,1)} async-done(((bf16[4,512,192]{1,2,0:T(8,128)(2,1)}), bf16[4,512,1536]{1,2,0:T(8,128)(2,1)}) %all-gather.4.cloned.1.call-update) | async-done | bytes 6291472 | tf_op jit(solution)/shard_map/all_gather | solution.py:81
  74.5 5.8 %convert_bitcast_fusion = bf16[4,512,1,448]{1,3,0,2:T(8,128)(2,1)S(1)} fusion(bf16[4,512,1536]{1,2,0:T(8,128)(2,1)} %all-gather.4.cloned.1.call-done, bf16[1536,448]{0,1:T(8,128)(2,1)S(1)} %copy-done), kind=kOutput, calls=%fused_computation.29 | convolution fusion | flops 2819489792 | bytes 9502720 | tf_op jit(solution)/shard_map/vtd,df->vtf/dot_general | solution.py:79
  84.1 3.0 stack.2
  87.1 6.7 %all-to-all-start = ((bf16[8,4,512,1,128]{4,2,1,3,0:T(8,128)(2,1)}), bf16[8,4,512,1,128]{4,2,1,3,0:T(8,128)(2,1)}, u32[]{:S(2)}, u32[]{:S(2)}) async-start(bf16[8,4,512,1,128]{4,2,1,3,0:T(8,128)(2,1)} %stack.2), calls=%async_computation | async-start | bytes 8388608 | tf_op jit(solution)/shard_map/all_to_all | solution.py:97
  94.1 56.4 %all-to-all-done = bf16[8,4,512,1,128]{4,2,1,3,0:T(8,128)(2,1)} async-done(((bf16[8,4,512,1,128]{4,2,1,3,0:T(8,128)(2,1)}), bf16[8,4,512,1,128]{4,2,1,3,0:T(8,128)(2,1)}, u32[]{:S(2)}, u32[]{:S(2)}) %all-to-all-start) | async-done | bytes 4194336 | tf_op jit(solution)/shard_map/all_to_all | solution.py:97
  150.5 4.7 %copy.38 = bf16[8,4,512,1,128]{4,2,0,1,3:T(8,128)(2,1)} copy(bf16[8,4,512,1,128]{4,2,1,3,0:T(8,128)(2,1)} %all-to-all-done) | data formatting | bytes 8388608 | tf_op jit(solution)/shard_map/all_to_all | solution.py:97
  155.2 60.9 %all-gather.6.cloned.1.call-done = bf16[4,4096,1,192]{1,3,0,2:T(8,128)(2,1)} async-done(((bf16[4,512,1,192]{1,3,0,2:T(8,128)(2,1)}), bf16[4,4096,1,192]{1,3,0,2:T(8,128)(2,1)}) %all-gather.6.cloned.1.call-update) | async-done | bytes 6291472 | tf_op jit(solution)/shard_map/all_gather | solution.py:99
  216.1 39.9 %while.18 = (s32[]{:T(128)}, f32[4,1,512]{2,0,1:T(4,128)S(1)}, f32[4,1,512]{2,0,1:T(4,128)S(1)}, f32[4,1,512,192]{2,3,0,1:T(8,128)S(1)}, bf16[4,4096,1,128]{3,1,...) while((s32[]{:T(128)}, f32[4,1,512]{2,0,1:T(4,128)S(1)}, ...), condition=%wide.region_3.4_spmd.clone, body=%wide.region_0.3_spmd.clone.sunk | while | flops 680669184 | bytes 17694904 | solution.py:55
  218.6 2.4 bitcast_add_fusion.5
  223.6 2.4 bitcast_add_fusion.5
  228.5 2.4 bitcast_add_fusion.5
  253.5 2.4 bitcast_add_fusion.5
  257.2 4.5 %fusion.19 = bf16[1536,2048]{0,1:T(8,128)(2,1)} fusion(bf16[2048,192]{0,1:T(8,128)(2,1)S(1)} %bitcast.99, bf16[192,1536]{1,0:T(8,128)(2,1)S(1)} %copy-done.5), kind=kOutput, calls=%fused_computation.26 | convolution fusion | flops 1211105280 | bytes 7667712 | tf_op jit(solution)/shard_map/dot_general | solution.py:105
  261.8 8.7 %copy.48 = bf16[1536,2048]{1,0:T(8,128)(2,1)} copy(bf16[1536,2048]{0,1:T(8,128)(2,1)} %fusion.19) | data formatting | bytes 12582912
  270.7 40.5 %reduce-scatter.4.cloned.1.call-done = bf16[192,2048]{1,0:T(8,128)(2,1)} async-done(((bf16[1536,2048]{1,0:T(8,128)(2,1)}), bf16[192,2048]{1,0:T(8,128)(2,1)}) %reduce-scatter.4.cloned.1.call-update) | async-done | bytes 786448
  314.2 2.9 copy.42
  317.1 3.6 convert_add_fusion
  324.7 59.8 %all-reduce.2.cloned.1.call-done = bf16[4,128,256]{2,1,0:T(8,128)(2,1)} async-done(((bf16[4,128,256]{2,1,0:T(8,128)(2,1)}), bf16[4,128,256]{2,1,0:T(8,128)(2,1)}) %all-reduce.2.cloned.1.call-update) | async-done | bytes 262160 | tf_op jit(solution)/shard_map/psum | solution.py:121
  386.3 8.9 %fusion.33 = f32[128,128,128]{2,1,0:T(8,128)} fusion(s32[128,128]{1,0:T(8,128)S(1)} %convert_add_fusion.1, f32[16,128]{1,0:T(8,128)S(1)} %copy-done.7), kind=kOutput, calls=%fused_computation.50 | convolution fusion | flops 402915328 | bytes 8462336 | tf_op jit(solution)/shard_map/dot_general | solution.py:138
  395.2 36.8 %all-gather.8.cloned.1.call-done = bf16[4,1024,128]{2,1,0:T(8,128)(2,1)} async-done(((bf16[4,128,128]{2,1,0:T(8,128)(2,1)}), bf16[4,1024,128]{2,1,0:T(8,128)(2,1)}) %all-gather.8.cloned.1.call-update) | async-done | bytes 1048592 | tf_op jit(solution)/shard_map/all_gather | solution.py:123
  433.0 12.4 %add_convert_fusion = bf16[4,128,128,128]{3,2,1,0:T(8,128)(2,1)} fusion(f32[128,128,128]{2,1,0:T(8,128)} %fusion.33, f32[4,128,128]{2,1,0:T(8,128)S(1)} %dynamic-slice_convert_fusion, f32[4,128,128]{2,1,0:T(8,128)S(1)} %get-tuple-element.213), kind=kLoop, calls=%fused_computation.24 | loop fusion | flops 25165824 | bytes 25690112 | tf_op jit(solution)/shard_map/convert_element_type | solution.py:140
  (103 shorter events, 52.3 us)
Async XLA Ops:
  6.5 68.0 %copy-start = (bf16[1536,448]{0,1:T(8,128)(2,1)S(1)}, bf16[1536,448]{0,1:T(8,128)(2,1)}, u32[]{:S(2)}) copy-start(bf16[1536,448]{0,1:T(8,128)(2,1)} %param.14) | copy-start | bytes 4128772
  6.5 6.9 %copy-start.9 = (f32[3,192]{1,0:T(4,128)S(1)}, f32[3,192]{1,0:T(4,128)}, u32[]{:S(2)}) copy-start(f32[3,192]{1,0:T(4,128)} %param.12) | copy-start | bytes 6916
  6.5 68.0 %all-gather.4.cloned.1.call-start = ((), (), s32[]{:S(2)}) async-start(), calls=%async_computation.2 | async-start | bytes 7077888 | tf_op jit(solution)/shard_map/all_gather | solution.py:81
  8.5 11.9 %collective-permute-start = (bf16[4,256,192]{1,2,0:T(8,128)(2,1)S(1)}, bf16[4,256,192]{1,2,0:T(8,128)(2,1)S(1)}, u32[]{:S(2)}, u32[]{:S(2)}) collective-permute-start(bf16[4,256,192]{1,2,0:T(8,128)(2,1)S(1)} %get-tuple-element.211), channel_id=1, source_target_pairs={{0,16},{16,32},{32,48},{48,64},{64,80},{80,96},{96,112},{1,17},{17... | collective-permute-start | bytes 1179656 | tf_op jit(solution)/shard_map/ppermute | solution.py:19
  12.1 12.5 %collective-permute-start.1 = (bf16[4,256,192]{1,2,0:T(8,128)(2,1)S(1)}, bf16[4,256,192]{1,2,0:T(8,128)(2,1)S(1)}, u32[]{:S(2)}, u32[]{:S(2)}) collective-permute-start(bf16[4,256,192]{1,2,0:T(8,128)(2,1)S(1)} %get-tuple-element.212), channel_id=1, source_target_pairs={{16,0},{32,16},{48,32},{64,48},{80,64},{96,80},{112,96},{17,1},{33... | collective-permute-start | bytes 1179656 | tf_op jit(solution)/shard_map/ppermute | solution.py:22
  13.4 13.4 %copy-start.8 = (f32[192]{0:T(256)S(1)}, f32[192]{0:T(256)}, u32[]{:S(2)}) copy-start(f32[192]{0:T(256)} %param.13) | copy-start | bytes 2308
  25.0 1.8 copy-start.2
  28.7 187.3 %all-gather.6.cloned.1.call-start = ((), (), s32[]{:S(2)}) async-start(), calls=%async_computation.3 | async-start | bytes 7077888 | tf_op jit(solution)/shard_map/all_gather | solution.py:99
  80.3 1.2 copy-start.4
  87.1 63.5 %all-to-all-start = ((bf16[8,4,512,1,128]{4,2,1,3,0:T(8,128)(2,1)}), bf16[8,4,512,1,128]{4,2,1,3,0:T(8,128)(2,1)}, u32[]{:S(2)}, u32[]{:S(2)}) async-start(bf16[8,4,512,1,128]{4,2,1,3,0:T(8,128)(2,1)} %stack.2), calls=%async_computation | async-start | bytes 8388608 | tf_op jit(solution)/shard_map/all_to_all | solution.py:97
  93.8 217.5 %reduce-scatter.4.cloned.1.call-start = ((), (), s32[]{:S(2)}) async-start(), calls=%async_computation.6 | async-start | bytes 7077888
  256.2 1.1 copy-start.5
  270.5 113.9 %all-reduce.2.cloned.1.call-start = ((), (), s32[]{:S(2)}) async-start(), calls=%async_computation.4 | async-start | bytes 524288 | tf_op jit(solution)/shard_map/psum | solution.py:121
  314.2 3.0 copy-start.3
  322.7 0.9 copy-start.6
  323.3 63.0 %copy-start.7 = (f32[16,128]{1,0:T(8,128)S(1)}, f32[16,128]{1,0:T(8,128)}, u32[]{:S(2)}) copy-start(f32[16,128]{1,0:T(8,128)} %param.17) | copy-start | bytes 24580
  324.6 107.4 %all-gather.8.cloned.1.call-start = ((), (), s32[]{:S(2)}) async-start(), calls=%async_computation.5 | async-start | bytes 1179648 | tf_op jit(solution)/shard_map/all_gather | solution.py:123
  433.0 12.4 %copy-start.1 = (bf16[1536,448]{0,1:T(8,128)(2,1)S(1)}, bf16[1536,448]{0,1:T(8,128)(2,1)}, u32[]{:S(2)}) copy-start(bf16[1536,448]{0,1:T(8,128)(2,1)} %param.14) | copy-start | bytes 4128772
Sparse Core Ops, SparseCore 0:
  28.9 45.5 all-gather.3
  82.6 133.4 all-gather.5
  270.6 40.5 reduce-scatter.3
  324.7 59.6 all-reduce.1
  386.8 45.1 all-gather.7
